TPU v7x, 32 devices: a whole 2x2x4 slice. The times are simulated.
32 devices in a mesh: loc: 4 (over z), ev: 8 (over y, x, core).
Axes of the slice: x: 2, y: 2, z: 4, core: 2. Of those that a mesh axis runs over, the one named last changes fastest.
Arguments:
- damage_noise: bfloat16 [1024, 32768], P('ev', 'loc'), may hold values from -4 to 4
- insured_value: float32 [32768], P('loc'), may hold values from 0.1 to 1
- policy_id: int32 [32768], P('loc'), may hold values from 0 to 4095
- bands: int32 [1024, 2], P('ev'), may hold values from 0 to 32768, as said below
- peak: float32 [1024], P('ev'), may hold values from 2 to 6
- event_year: int32 [1024], P('ev'), may hold values from 0 to 255, as said below
- deductible: float32 [4096], replicated, may hold values from 0.05 to 0.5
- limit: float32 [4096], replicated, may hold values from 0.5 to 2
- levels: int32 [32], replicated, may hold values from 0 to 149
Outputs:
- annual_loss: float32 [256], P('ev')
- occurrence_loss: float32 [256], P('ev')
- aggregate_curve: float32 [32], replicated
- occurrence_curve: float32 [32], replicated
Inputs may be any that keep to these rules, and one draw needn't show every extreme that they name: bands[e,0] < bands[e,1]; each band spans 2048 to 16384 locations. `event_year`: among the 128 events of one index of ev, at most 32 have years in any one index's block of 32 years (years j * 32 to (j + 1) * 32 - 1); in every draw some block of years receives exactly 32 events from every index of ev.
All inputs are finite; a program needn't handle non-finite values.
Results may differ from a plain program's by a relative error of at most 0.0003.
Values sent between devices are 32-bit elements; how exact they have to be, the bound alone decides.
A program may use at most 64 MiB of HBM per device.

v0:
```python
import jax
import jax.numpy as jnp
from jax import lax
from jax.sharding import PartitionSpec as P

YR_DEV = 32


def ground_losses(damage_noise, insured_value, bands, peak, anchor):
    amount = insured_value.shape[0]
    position = (anchor + lax.iota(jnp.int32, amount)).astype(jnp.float32) + 0.5
    band_low = bands[:, 0].astype(jnp.float32)
    band_high = bands[:, 1].astype(jnp.float32)
    center = 0.5 * (band_low + band_high)
    half_width = 0.5 * (band_high - band_low)
    offset = (position[None, :] - center[:, None]) / half_width[:, None]
    wind_speed = peak[:, None] * jnp.maximum(1.0 - offset * offset, 0.0)
    cube_wind = wind_speed * wind_speed * wind_speed
    damage_ratio = cube_wind / (cube_wind + 1.0)
    factor = jnp.exp(0.5 * damage_noise.astype(jnp.float32) - 0.125)
    return (insured_value[None, :] * damage_ratio * factor).astype(jnp.bfloat16)


def policy_rows(ground, policy_id, row_count):
    location_count = ground.shape[1]
    block_size = min(1024, location_count)
    wanted = lax.iota(jnp.int32, row_count)

    def accumulate(block_index, running):
        offset_start = block_index * block_size
        ground_block = lax.dynamic_slice_in_dim(ground, offset_start, block_size, 1)
        owner_block = lax.dynamic_slice_in_dim(policy_id, offset_start, block_size, 0)
        one_hot = (owner_block[:, None] == wanted[None, :]).astype(jnp.bfloat16)
        return running + lax.dot_general(
            one_hot, ground_block, (((0,), (1,)), ((), ())), preferred_element_type=jnp.float32
        )

    return lax.fori_loop(
        0,
        location_count // block_size,
        accumulate,
        jnp.zeros((row_count, ground.shape[0]), jnp.float32),
    )


def excess_sum(losses, thresholds):
    return jnp.sum(jnp.maximum(losses[:, None] - thresholds[None, :], 0.0), axis=0)


def event_sums(shares, deductible_share, limit_share, policies):
    trailing = (-1,) + (1,) * (shares.ndim - 1)
    net = jnp.minimum(
        jnp.maximum(shares - deductible_share.reshape(trailing), 0.0), limit_share.reshape(trailing)
    )
    policy_part = jnp.sum(net, axis=0).reshape(-1)
    return lax.psum(policy_part, "loc") / policies


def local(
    damage_noise, insured_value, policy_id, bands, peak, event_year, deductible, limit, levels
):
    events_here = damage_noise.shape[0]
    policies = deductible.shape[0]
    owner_count = lax.axis_size("ev")
    capacity = 2 * events_here // owner_count
    slot_count = owner_count * capacity
    share_width = policies // lax.axis_size("loc")
    anchor = lax.axis_index("loc") * insured_value.shape[0]
    ground = ground_losses(damage_noise, insured_value, bands, peak, anchor)
    owners = event_year // YR_DEV
    year_code = (event_year - owners * YR_DEV + 1).astype(jnp.float32)
    same_owner = owners[:, None] == owners[None, :]
    before = lax.iota(jnp.int32, events_here)[:, None] > lax.iota(jnp.int32, events_here)[None, :]
    ranking = jnp.sum((same_owner & before).astype(jnp.int32), axis=1)
    slot_index = owners * capacity + ranking
    placing = (slot_index[:, None] == lax.iota(jnp.int32, slot_count)[None, :]).astype(jnp.float32)
    slot_codes = jnp.dot(year_code[None, :], placing, precision=lax.Precision.HIGHEST).reshape(
        1, owner_count, capacity
    )
    first_policy = lax.axis_index("loc") * share_width
    deductible_share = lax.dynamic_slice_in_dim(deductible, first_policy, share_width, 0)
    limit_share = lax.dynamic_slice_in_dim(limit, first_policy, share_width, 0)
    gross = policy_rows(ground, policy_id, policies)
    spread = jnp.dot(gross, placing, precision=lax.Precision.HIGHEST)
    moved = lax.all_to_all(
        spread.reshape(gross.shape[0], owner_count, capacity),
        "ev",
        split_axis=1,
        concat_axis=1,
        tiled=True,
    )
    arrived = lax.all_to_all(slot_codes, "ev", split_axis=1, concat_axis=1, tiled=True)
    shares = lax.psum_scatter(moved, "loc", scatter_dimension=0, tiled=True)
    event_loss = event_sums(shares, deductible_share, limit_share, policies)
    year_ids = arrived.reshape(slot_count)
    matches = year_ids[:, None] == (lax.iota(jnp.int32, YR_DEV) + 1).astype(jnp.float32)[None, :]
    masked = jnp.where(matches, event_loss[:, None], 0.0)
    annual_loss = jnp.sum(masked, axis=0)
    occurrence_loss = jnp.max(masked, axis=0)
    thresholds = levels.astype(jnp.float32) / 100.0
    year_total = YR_DEV * owner_count
    aggregate_sum, occurrence_sum = lax.psum(
        (excess_sum(annual_loss, thresholds), excess_sum(occurrence_loss, thresholds)), "ev"
    )
    return (annual_loss, occurrence_loss, aggregate_sum / year_total, occurrence_sum / year_total)


def solution(mesh):
    placed = (P("ev", "loc"), P("loc"), P("loc"), P("ev", None), P("ev"), P("ev"), P(), P(), P())
    return jax.shard_map(
        local, mesh=mesh, in_specs=placed, out_specs=(P("ev"), P("ev"), P(), P()), check_vma=False
    )
```

profile of v0, /device:TPU:0, one launch (start us, length us, event | category | flops | bytes accessed | tf_op | source)
XLA Modules:
  0.0 217.5 jit_solution(14918330165965624885)
XLA Ops:
  7.2 0.0 reduce-scatter.2.cloned.1.call-start
  7.2 0.8 multiply_bitcast_fusion.1
  8.0 5.0 %fusion.13 = bf16[128,8192]{1,0:T(8,128)(2,1)} fusion(bf16[128,8192]{1,0:T(8,128)(2,1)} %param.11, f32[128]{0:T(128)S(1)} %get-tuple-element.131, f32[128]{0:T(128)S(1)} %get-tuple-element.130, f32[8192]{0:T(1024)S(1)} %convert_add_fusion, f32[128]{0:T(128)} %param.15, f32[8192]{0:T(1024)} %param.12), kind=kLoop, calls=%fused_computation.12 | loop fusion | flops 16777216 | bytes 4261376 | tf_op jit(solution)/shard_map/convert_element_type | solution.py:21
  13.0 0.0 copy-start.2
  13.0 39.9 %while.14 = (s32[]{:T(128)}, f32[4096,128]{1,0:T(8,128)S(1)}, s32[8192]{0:T(1024)}, bf16[128,8192]{1,0:T(8,128)(2,1)}, s32[]{:T(128)}, /*index=5*/s32[]{:T(128)}, s32[]{:T(128)}, s32[]{:T(128)}) while((s32[]{:T(128)}, f32[4096,128]{1,0:T(8,128)S(1)}, s32[8192]{0:T(1024)}, bf16[128,8192]{1,0:T(8,128)(2,1)}, s32[]{:T(128)}, ...), condition=%wide.region_2.3_spmd.clone, body=%wide.region_1.2_spmd.clone.sunk | while | flops 1083179008 | bytes 4468893 | solution.py:38
  13.0 0.7 dynamic_slice.29
  13.7 4.3 %fusion.34 = f32[4096,128]{1,0:T(8,128)S(1)} fusion(s32[1024]{0:T(1024)S(1)} %dynamic_slice.29, f32[4096,128]{1,0:T(8,128)S(1)} %get-tuple-element.168, pred[]{:T(512)S(6)} %compare.5, bf16[128,8192]{1,0:T(8,128)(2,1)} %get-tuple-element.178, s32[]{:T(128)S(6)} %select_n.31), kind=kOutput, calls=%fused_computation.5.clone.1 | convolution fusion | flops 1083179008 | bytes 4460549 | tf_op jit(solution)/shard_map/while/body/eval_jaxpr/dot_general | solution.py:34
  18.0 0.7 dynamic_slice.29
  18.7 4.3 %fusion.34 = f32[4096,128]{1,0:T(8,128)S(1)} fusion(s32[1024]{0:T(1024)S(1)} %dynamic_slice.29, f32[4096,128]{1,0:T(8,128)S(1)} %get-tuple-element.168, pred[]{:T(512)S(6)} %compare.5, bf16[128,8192]{1,0:T(8,128)(2,1)} %get-tuple-element.178, s32[]{:T(128)S(6)} %select_n.31), kind=kOutput, calls=%fused_computation.5.clone.1 | convolution fusion | flops 1083179008 | bytes 4460549 | tf_op jit(solution)/shard_map/while/body/eval_jaxpr/dot_general | solution.py:34
  23.0 0.7 dynamic_slice.29
  23.7 4.3 %fusion.34 = f32[4096,128]{1,0:T(8,128)S(1)} fusion(s32[1024]{0:T(1024)S(1)} %dynamic_slice.29, f32[4096,128]{1,0:T(8,128)S(1)} %get-tuple-element.168, pred[]{:T(512)S(6)} %compare.5, bf16[128,8192]{1,0:T(8,128)(2,1)} %get-tuple-element.178, s32[]{:T(128)S(6)} %select_n.31), kind=kOutput, calls=%fused_computation.5.clone.1 | convolution fusion | flops 1083179008 | bytes 4460549 | tf_op jit(solution)/shard_map/while/body/eval_jaxpr/dot_general | solution.py:34
  28.0 0.7 dynamic_slice.29
  28.6 4.3 %fusion.34 = f32[4096,128]{1,0:T(8,128)S(1)} fusion(s32[1024]{0:T(1024)S(1)} %dynamic_slice.29, f32[4096,128]{1,0:T(8,128)S(1)} %get-tuple-element.168, pred[]{:T(512)S(6)} %compare.5, bf16[128,8192]{1,0:T(8,128)(2,1)} %get-tuple-element.178, s32[]{:T(128)S(6)} %select_n.31), kind=kOutput, calls=%fused_computation.5.clone.1 | convolution fusion | flops 1083179008 | bytes 4460549 | tf_op jit(solution)/shard_map/while/body/eval_jaxpr/dot_general | solution.py:34
  32.9 0.7 dynamic_slice.29
  33.6 4.3 %fusion.34 = f32[4096,128]{1,0:T(8,128)S(1)} fusion(s32[1024]{0:T(1024)S(1)} %dynamic_slice.29, f32[4096,128]{1,0:T(8,128)S(1)} %get-tuple-element.168, pred[]{:T(512)S(6)} %compare.5, bf16[128,8192]{1,0:T(8,128)(2,1)} %get-tuple-element.178, s32[]{:T(128)S(6)} %select_n.31), kind=kOutput, calls=%fused_computation.5.clone.1 | convolution fusion | flops 1083179008 | bytes 4460549 | tf_op jit(solution)/shard_map/while/body/eval_jaxpr/dot_general | solution.py:34
  37.9 0.7 dynamic_slice.29
  38.6 4.3 %fusion.34 = f32[4096,128]{1,0:T(8,128)S(1)} fusion(s32[1024]{0:T(1024)S(1)} %dynamic_slice.29, f32[4096,128]{1,0:T(8,128)S(1)} %get-tuple-element.168, pred[]{:T(512)S(6)} %compare.5, bf16[128,8192]{1,0:T(8,128)(2,1)} %get-tuple-element.178, s32[]{:T(128)S(6)} %select_n.31), kind=kOutput, calls=%fused_computation.5.clone.1 | convolution fusion | flops 1083179008 | bytes 4460549 | tf_op jit(solution)/shard_map/while/body/eval_jaxpr/dot_general | solution.py:34
  42.9 0.7 dynamic_slice.29
  43.6 4.3 %fusion.34 = f32[4096,128]{1,0:T(8,128)S(1)} fusion(s32[1024]{0:T(1024)S(1)} %dynamic_slice.29, f32[4096,128]{1,0:T(8,128)S(1)} %get-tuple-element.168, pred[]{:T(512)S(6)} %compare.5, bf16[128,8192]{1,0:T(8,128)(2,1)} %get-tuple-element.178, s32[]{:T(128)S(6)} %select_n.31), kind=kOutput, calls=%fused_computation.5.clone.1 | convolution fusion | flops 1083179008 | bytes 4460549 | tf_op jit(solution)/shard_map/while/body/eval_jaxpr/dot_general | solution.py:34
  47.9 0.7 dynamic_slice.29
  48.6 4.3 %fusion.34 = f32[4096,128]{1,0:T(8,128)S(1)} fusion(s32[1024]{0:T(1024)S(1)} %dynamic_slice.29, f32[4096,128]{1,0:T(8,128)S(1)} %get-tuple-element.168, pred[]{:T(512)S(6)} %compare.5, bf16[128,8192]{1,0:T(8,128)(2,1)} %get-tuple-element.178, s32[]{:T(128)S(6)} %select_n.31), kind=kOutput, calls=%fused_computation.5.clone.1 | convolution fusion | flops 1083179008 | bytes 4460549 | tf_op jit(solution)/shard_map/while/body/eval_jaxpr/dot_general | solution.py:34
  52.9 0.0 copy-done.2
  52.9 0.2 convert_reduce_fusion
  53.1 2.0 fusion.14
  55.1 54.1 %all_to_all.10 = f32[4096,8,32]{0,2,1:T(8,128)} all-to-all(f32[4096,8,32]{0,2,1:T(8,128)S(1)} %bitcast.12), channel_id=1, replica_groups=mesh['loc'=4,'ev'=8] {'ev'}, dimensions={1} | all-to-all | bytes 8388608 | tf_op jit(solution)/shard_map/all_to_all | solution.py:85
  109.3 0.0 copy-start.3
  109.3 0.0 reduce-scatter.2.cloned.1.call-update
  109.3 1.0 fusion.15
  110.3 3.3 %all-to-all-start = ((f32[1,8,32]{2,0,1:T(1,128)}), f32[1,8,32]{2,0,1:T(1,128)S(1)}, u32[]{:S(2)}, u32[]{:S(2)}) async-start(f32[1,8,32]{2,0,1:T(1,128)} %fusion.15), calls=%async_computation | async-start | bytes 8192 | tf_op jit(solution)/shard_map/all_to_all | solution.py:92
  113.6 0.0 copy-done.3
  113.6 0.7 dynamic_slice.21
  114.3 0.7 dynamic_slice.20
  115.0 3.2 %all-to-all-done = f32[1,8,32]{2,0,1:T(1,128)S(1)} async-done(((f32[1,8,32]{2,0,1:T(1,128)}), f32[1,8,32]{2,0,1:T(1,128)S(1)}, u32[]{:S(2)}, u32[]{:S(2)}) %all-to-all-start) | async-done | bytes 1056 | tf_op jit(solution)/shard_map/all_to_all | solution.py:92
  118.2 0.5 broadcast.95
  118.7 0.7 reduce.3
  119.4 0.1 eq.103
  119.5 66.1 %reduce-scatter.2.cloned.1.call-done = f32[1024,8,32]{0,2,1:T(8,128)} async-done(((f32[4096,8,32]{0,2,1:T(8,128)}), f32[1024,8,32]{0,2,1:T(8,128)}) %reduce-scatter.2.cloned.1.call-update) | async-done | bytes 1048592 | tf_op jit(solution)/shard_map/reduce_scatter | solution.py:93
  185.6 1.4 minimum_reduce_fusion
  187.0 0.1 reshape.64
  187.1 10.9 %psum.21 = f32[256]{0:T(256)S(1)} all-reduce(f32[256]{0:T(256)S(1)} %reshape.64), channel_id=1, replica_groups=mesh['loc'=4,'ev'=8] {'loc'}, use_global_device_ids=true, to_apply=%region_5.6 | all-reduce | flops 256 | bytes 2048 | tf_op jit(solution)/shard_map/psum | solution.py:56
  198.0 0.2 select_reduce_fusion
  198.2 0.0 copy-start
  198.2 0.0 copy-start.1
  198.2 0.1 maximum_reduce_fusion
  198.3 11.9 %all-reduce = (f32[32]{0:T(128)S(1)}, f32[32]{0:T(128)S(1)}) all-reduce(f32[32]{0:T(128)S(1)} %get-tuple-element.119, f32[32]{0:T(128)S(1)} %get-tuple-element.118), channel_id=1, replica_groups=mesh['loc'=4,'ev'=8] {'ev'}, use_global_device_ids=true, to_apply=%region_9.10 | all-reduce | flops 64 | bytes 512 | tf_op jit(solution)/shard_map/psum | solution.py:102
  210.2 0.5 broadcast_multiply_fusion.1
  210.7 0.0 copy-done
  210.7 0.0 copy-done.1
  (8 shorter events, 0.1 us)
Async XLA Ops:
  7.2 178.4 %reduce-scatter.2.cloned.1.call-start = ((), (), s32[]{:S(2)}) async-start(), calls=%async_computation.3 | async-start | bytes 5242880 | tf_op jit(solution)/shard_map/reduce_scatter | solution.py:93
  13.0 40.0 %copy-start.2 = (s32[128]{0:T(128)S(1)}, s32[128]{0:T(128)}, u32[]{:S(2)}) copy-start(s32[128]{0:T(128)} %param.16) | copy-start | bytes 1540
  109.3 4.4 %copy-start.3 = (s32[32]{0:T(128)S(1)}, s32[32]{0:T(128)}, u32[]{:S(2)}) copy-start(s32[32]{0:T(128)} %param.19) | copy-start | bytes 388
  110.3 7.9 %all-to-all-start = ((f32[1,8,32]{2,0,1:T(1,128)}), f32[1,8,32]{2,0,1:T(1,128)S(1)}, u32[]{:S(2)}, u32[]{:S(2)}) async-start(f32[1,8,32]{2,0,1:T(1,128)} %fusion.15), calls=%async_computation | async-start | bytes 8192 | tf_op jit(solution)/shard_map/all_to_all | solution.py:92
  198.2 12.5 %copy-start = (f32[32]{0:T(128)}, f32[32]{0:T(128)S(1)}, u32[]{:S(2)}) copy-start(f32[32]{0:T(128)S(1)} %get-tuple-element.116) | copy-start | bytes 388
  198.2 12.5 %copy-start.1 = (f32[32]{0:T(128)}, f32[32]{0:T(128)S(1)}, u32[]{:S(2)}) copy-start(f32[32]{0:T(128)S(1)} %get-tuple-element.117) | copy-start | bytes 388
Sparse Core Ops, SparseCore 0:
  109.4 76.1 reduce-scatter.1
where the time goes:
time: 218 us
  blocking collectives  76.9 us (35%)
  waiting for transfers between devices  69.3 us (32%)
  matrix products  37.2 us (17%)
  between operations  14.2 us (7%)
  other arithmetic  8.84 us (4%)
  local copies, waits for them, and re-layouts  7.63 us (4%)
  starting transfers between devices  3.32 us (2%)
    reduce_scatter x1, waiting for transfers between devices, local(): shares = lax.psum_scatter(moved, 'loc', scatter_dimension=0, tiled=True)  66.1 us
    all_to_all x1, blocking collectives, local(): lax.all_to_all(spread.reshape(gross.shape[0], owner_count, capacity), 'ev...  54.1 us
    dot_general x8, matrix products, accumulate(): lax.dot_general(one_hot, ground_block, (((0,), (1,)), ((), ())), preferre...  34.2 us
    psum x1, blocking collectives, local(): lax.psum((excess_sum(annual_loss, thresholds), excess_sum(occurrence_loss...  11.9 us
    psum x1, blocking collectives, event_sums(): return lax.psum(policy_part, 'loc') / policies  10.9 us
    dynamic_slice x8, local copies, waits for them, and re-layouts, accumulate(): lax.dynamic_slice_in_dim(policy_id, offset_start, block_size, 0)  5.55 us
    convert_element_type x1, other arithmetic, ground_losses(): return (insured_value[None, :] * damage_ratio * factor).astype(jnp.bfloat16)  4.96 us
  transfers between devices with their start and end apart: 2, of which 2 were waited for; matrix products, arithmetic and copies ran while one was open for 2% of the time, Pallas kernels for 0%

commit v1 on v0

v1 whole, which is shorter than its diff:
```python
import functools

import jax
import jax.numpy as jnp
from jax import lax
from jax.experimental import pallas as pl
from jax.experimental.pallas import tpu as pltpu
from jax.sharding import PartitionSpec as P

YR_DEV = 32
LANES = 128
LOW = 256
GROUP = 16
CHUNK = 1024
LAG = 1


def kernel(
    axes, noise, insured, policy, bands, peak, year, deductible, limit, levels,
    annual_out, occurrence_out, aggregate_out, excess_out,
    block_mask, column_mask, center, inverse, strength, own, arrived, net_sum, halves, rows,
    annual_all, occurrence_all,
    send_sem, recv_sem, half_send, half_recv, row_send, row_recv,
):
    depth, owners = axes
    z = lax.axis_index("loc")
    ev = lax.axis_index("ev")
    events, locations = noise.shape
    policies = deductible.shape[0] * LANES
    blocks = policies // LOW
    half_blocks = blocks // 2
    groups = events // GROUP
    chunks = locations // CHUNK
    half_rows = half_blocks * GROUP

    barrier = pltpu.get_barrier_semaphore()
    for k in range(1, depth):
        pl.semaphore_signal(barrier, inc=1, device_id={"loc": lax.rem(z + k, depth)})
    for k in range(1, owners):
        pl.semaphore_signal(barrier, inc=1, device_id={"ev": lax.rem(ev + k, owners)})

    low = jnp.transpose(jnp.broadcast_to(bands[0:1, :].astype(jnp.float32), (LANES, events)))
    high = jnp.transpose(jnp.broadcast_to(bands[1:2, :].astype(jnp.float32), (LANES, events)))
    center[...] = 0.5 * (low + high)
    inverse[...] = 1.0 / (0.5 * (high - low))
    strength[...] = jnp.transpose(jnp.broadcast_to(peak[...], (LANES, events)))

    def build(c, carry):
        at = pl.ds(pl.multiple_of(c * CHUNK, CHUNK), CHUNK)
        ids = policy[:, at]
        column = jnp.broadcast_to(ids & (LOW - 1), (LOW, CHUNK))
        wanted = lax.broadcasted_iota(jnp.int32, (LOW, CHUNK), 0)
        column_mask[:, at] = jnp.where(column == wanted, 1.0, 0.0).astype(jnp.bfloat16)
        block = jnp.broadcast_to(ids >> 8, (GROUP, CHUNK))
        for b in range(blocks):
            block_mask[b * GROUP : (b + 1) * GROUP, at] = jnp.where(block == b, 1.0, 0.0).astype(
                jnp.bfloat16
            )
        return carry

    lax.fori_loop(0, chunks, build, 0)
    pl.semaphore_wait(barrier, depth - 1 + owners - 1)

    anchor = z * locations
    wide = CHUNK // LANES

    def compute(g):
        which = pl.ds(pl.multiple_of(g * GROUP, GROUP), GROUP)
        mid = jnp.concatenate([center[which, :]] * wide, axis=1)
        inv = jnp.concatenate([inverse[which, :]] * wide, axis=1)
        top = jnp.concatenate([strength[which, :]] * wide, axis=1)

        def part(c, total):
            start = pl.multiple_of(c * CHUNK, CHUNK)
            at = pl.ds(start, CHUNK)
            place = lax.broadcasted_iota(jnp.int32, (GROUP, CHUNK), 1) + (anchor + start)
            offset = (place.astype(jnp.float32) + 0.5 - mid) * inv
            wind = top * jnp.maximum(1.0 - offset * offset, 0.0)
            cube = wind * wind * wind
            factor = jnp.exp(0.5 * noise[which, at].astype(jnp.float32) - 0.125)
            ground = (insured[:, at] * (cube / (cube + 1.0)) * factor).astype(jnp.bfloat16)
            left = jnp.concatenate([ground] * blocks, axis=0) * block_mask[:, at]
            return total + lax.dot_general(
                left, column_mask[:, at], (((1,), (1,)), ((), ())),
                preferred_element_type=jnp.float32,
            )

        total = lax.fori_loop(0, chunks, part, jnp.zeros((blocks * GROUP, LOW), jnp.float32))
        own[0, g] = total[:half_rows]
        own[1, g] = total[half_rows:]

    def hop(d, g, there):
        return pltpu.make_async_remote_copy(
            src_ref=own.at[d, g], dst_ref=arrived.at[d, g],
            send_sem=send_sem.at[d, g], recv_sem=recv_sem.at[d, g],
            device_id={"loc": there},
        )

    def settle(d, g):
        total = jnp.zeros((GROUP, LANES), jnp.float32)
        for b in range(half_blocks):
            for j in range(LOW // LANES):
                row = (d * half_blocks + b) * (LOW // LANES) + j
                gross = own[d, g, b * GROUP : (b + 1) * GROUP, j * LANES : (j + 1) * LANES]
                net = jnp.maximum(gross - deductible[row : row + 1, :], 0.0)
                total = total + jnp.minimum(net, limit[row : row + 1, :])
        net_sum[pl.ds(pl.multiple_of(g * GROUP, GROUP), GROUP), :] = total

    def step(s, carry):
        @pl.when(s < groups)
        def _():
            compute(s)

        for d in (0, 1):
            gone = z if d == 1 else depth - 1 - z
            there = jnp.minimum(z + 1, depth - 1) if d == 1 else jnp.maximum(z - 1, 0)
            g = s - LAG * gone
            active = (g >= 0) & (g < groups)

            @pl.when(active & (gone > 0))
            def _():
                hop(d, g, there).wait_recv()
                own[d, g] = own[d, g] + arrived[d, g]

            @pl.when(active & (gone < depth - 1))
            def _():
                hop(d, g, there).start()

            @pl.when(active & (gone == depth - 1))
            def _():
                settle(d, g)

        return carry

    lax.fori_loop(0, groups + LAG * (depth - 1), step, 0)

    def half_copy(d, k):
        return pltpu.make_async_remote_copy(
            src_ref=halves.at[d], dst_ref=halves.at[d],
            send_sem=half_send.at[k], recv_sem=half_recv.at[d],
            device_id={"loc": lax.rem(z + k, depth)},
        )

    for d in (0, 1):
        owner = 0 if d == 0 else depth - 1

        @pl.when(z == owner)
        def _():
            row = jnp.sum(jnp.transpose(net_sum[...]), axis=0, keepdims=True)
            halves[d] = jnp.broadcast_to(row, (8, events))
            for k in range(1, depth):
                half_copy(d, k).start()

    for d in (0, 1):
        owner = 0 if d == 0 else depth - 1

        @pl.when(z != owner)
        def _():
            half_copy(d, 1).wait_recv()

    loss = (halves[0] + halves[1]) / policies
    first = lax.broadcasted_iota(jnp.int32, (8, events), 0) == 0
    rows[ev] = jnp.where(first, loss, jnp.broadcast_to(year[...].astype(jnp.float32), (8, events)))

    def row_copy(k, slot):
        return pltpu.make_async_remote_copy(
            src_ref=rows.at[slot], dst_ref=rows.at[slot],
            send_sem=row_send.at[k], recv_sem=row_recv.at[k],
            device_id={"ev": lax.rem(ev + k, owners)},
        )

    for k in range(1, owners):
        row_copy(k, ev).start()
    for k in range(1, owners):
        row_copy(k, lax.rem(ev - k + owners, owners)).wait_recv()

    years = YR_DEV * owners
    span = 64
    threshold = levels[...].astype(jnp.float32) / 100.0

    def tally(c, sums):
        start = pl.multiple_of(c * span, span)
        label = (lax.broadcasted_iota(jnp.int32, (span, events), 0) + start).astype(jnp.float32)
        annual = jnp.zeros((span, events), jnp.float32)
        largest = jnp.zeros((span, events), jnp.float32)
        for r in range(owners):
            block = rows[r]
            hit = jnp.where(label == block[1:2, :], block[0:1, :], 0.0)
            annual = annual + hit
            largest = jnp.maximum(largest, hit)
        annual = jnp.sum(annual, axis=1, keepdims=True)
        largest = jnp.max(largest, axis=1, keepdims=True)
        annual_all[pl.ds(start, span), :] = jnp.broadcast_to(annual, (span, LANES))
        occurrence_all[pl.ds(start, span), :] = jnp.broadcast_to(largest, (span, LANES))
        return (
            sums[0] + jnp.sum(jnp.maximum(annual - threshold, 0.0), axis=0, keepdims=True),
            sums[1] + jnp.sum(jnp.maximum(largest - threshold, 0.0), axis=0, keepdims=True),
        )

    zero = jnp.zeros(levels.shape, jnp.float32)
    sums = lax.fori_loop(0, years // span, tally, (zero, zero))
    aggregate_out[...] = sums[0] / years
    excess_out[...] = sums[1] / years

    mine = pl.ds(pl.multiple_of(ev * YR_DEV, YR_DEV), YR_DEV)
    diagonal = lax.broadcasted_iota(jnp.int32, (YR_DEV, LANES), 0) == lax.broadcasted_iota(
        jnp.int32, (YR_DEV, LANES), 1
    )
    for out, every in ((annual_out, annual_all), (occurrence_out, occurrence_all)):
        row = jnp.sum(jnp.where(diagonal, every[mine, :], 0.0), axis=0, keepdims=True)
        out[...] = row[:, :YR_DEV]

    def drain(g, carry):
        for d in (0, 1):
            gone = z if d == 1 else depth - 1 - z

            @pl.when(gone < depth - 1)
            def _():
                hop(d, g, jnp.minimum(z + 1, depth - 1) if d == 1 else jnp.maximum(z - 1, 0)).wait_send()

        return carry

    lax.fori_loop(0, groups, drain, 0)
    for d in (0, 1):
        owner = 0 if d == 0 else depth - 1

        @pl.when(z == owner)
        def _():
            for k in range(1, depth):
                half_copy(d, k).wait_send()

    for k in range(1, owners):
        row_copy(k, ev).wait_send()


def local(
    damage_noise, insured_value, policy_id, bands, peak, event_year, deductible, limit, levels
):
    depth, owners = lax.axis_size("loc"), lax.axis_size("ev")
    events, locations = damage_noise.shape
    policies = deductible.shape[0]
    thresholds = levels.shape[0]
    blocks = policies // LOW
    groups = events // GROUP
    half_rows = blocks // 2 * GROUP
    years = YR_DEV * owners
    row = jax.ShapeDtypeStruct((1, YR_DEV), jnp.float32)
    curve = jax.ShapeDtypeStruct((1, thresholds), jnp.float32)
    vmem = pl.BlockSpec(memory_space=pltpu.VMEM)
    outs = pl.pallas_call(
        functools.partial(kernel, (depth, owners)),
        out_shape=(row, row, curve, curve),
        in_specs=[vmem] * 9,
        out_specs=(vmem,) * 4,
        scratch_shapes=[
            pltpu.VMEM((blocks * GROUP, locations), jnp.bfloat16),
            pltpu.VMEM((LOW, locations), jnp.bfloat16),
            pltpu.VMEM((events, LANES), jnp.float32),
            pltpu.VMEM((events, LANES), jnp.float32),
            pltpu.VMEM((events, LANES), jnp.float32),
            pltpu.VMEM((2, groups, half_rows, LOW), jnp.float32),
            pltpu.VMEM((2, groups, half_rows, LOW), jnp.float32),
            pltpu.VMEM((events, LANES), jnp.float32),
            pltpu.VMEM((2, 8, events), jnp.float32),
            pltpu.VMEM((owners, 8, events), jnp.float32),
            pltpu.VMEM((years, LANES), jnp.float32),
            pltpu.VMEM((years, LANES), jnp.float32),
            pltpu.SemaphoreType.DMA((2, groups)),
            pltpu.SemaphoreType.DMA((2, groups)),
            pltpu.SemaphoreType.DMA((depth,)),
            pltpu.SemaphoreType.DMA((2,)),
            pltpu.SemaphoreType.DMA((owners,)),
            pltpu.SemaphoreType.DMA((owners,)),
        ],
        compiler_params=pltpu.CompilerParams(
            collective_id=0, has_side_effects=True, vmem_limit_bytes=48 * 1024 * 1024
        ),
    )(
        damage_noise,
        insured_value.reshape(1, locations),
        policy_id.reshape(1, locations),
        bands.T,
        peak.reshape(1, events),
        event_year.reshape(1, events),
        deductible.reshape(policies // LANES, LANES),
        limit.reshape(policies // LANES, LANES),
        levels.reshape(1, thresholds),
    )
    return tuple(out.reshape(-1) for out in outs)


def solution(mesh):
    placed = (P("ev", "loc"), P("loc"), P("loc"), P("ev", None), P("ev"), P("ev"), P(), P(), P())
    return jax.shard_map(
        local, mesh=mesh, in_specs=placed, out_specs=(P("ev"), P("ev"), P(), P()), check_vma=False
    )
```

time: 218 us -> 69.1 us (0.32)
  blocking collectives: 76.9 us -> 0 us
  waiting for transfers between devices: 69.3 us -> 0 us
  Pallas kernels: 0 us -> 58.8 us
  matrix products: 37.2 us -> 0 us
  between operations: 14.2 us -> 0.66 us
  other arithmetic: 8.84 us -> 0 us
  starting transfers between devices: 3.32 us -> 0 us
    reduce_scatter x1 -> x0, waiting for transfers between devices: 66.1 us -> none  [local(): shares = lax.psum_scatter(moved, 'loc', scatter_dimension=0, tiled=True)]
    pallas_call x0 -> x1, Pallas kernels: none -> 58.8 us  [local(): pl.pallas_call(functools.partial(kernel, (depth, owners)), out_shape=(row...]
    all_to_all x1 -> x0, blocking collectives: 54.1 us -> none  [local(): lax.all_to_all(spread.reshape(gross.shape[0], owner_count, capacity), 'ev...]
    dot_general x10 -> x0, matrix products: 37.2 us -> none  [the longest x8 34.2 us: accumulate(): lax.dot_general(one_hot, ground_block, (((0,), (1,)), ((), ())), preferre...]
    psum x2 -> x0, blocking collectives: 22.8 us -> none  [the longest x1 11.9 us: local(): lax.psum((excess_sum(annual_loss, thresholds), excess_sum(occurrence_loss...]
    unnamed x8 -> x22, local copies, waits for them, and re-layouts: 0.02 us -> 9.22 us
    dynamic_slice x10 -> x0, local copies, waits for them, and re-layouts: 6.94 us -> none  [the longest x8 5.55 us: accumulate(): lax.dynamic_slice_in_dim(policy_id, offset_start, block_size, 0)]
    convert_element_type x2 -> x0, other arithmetic: 4.97 us -> none  [the longest x1 4.96 us: ground_losses(): return (insured_value[None, :] * damage_ratio * factor).astype(jnp.bfloat16)]
  transfers between devices with their start and end apart: 2 -> 0, of which waited for: 2 -> 0; matrix products, arithmetic and copies ran while one was open for 2% -> 0% of each run, Pallas kernels for 0% -> 0%
where the time goes in v1:
time: 69.1 us; the launch traced here: 68.7 us
  Pallas kernels  58.8 us (85%)
  local copies, waits for them, and re-layouts  9.22 us (13%)
    pallas_call x1, Pallas kernels, local(): pl.pallas_call(functools.partial(kernel, (depth, owners)), out_shape=(row...  58.8 us
    unnamed x22, local copies, waits for them, and re-layouts  9.22 us

profile of v1, /device:TPU:0, one launch (start us, length us, event | category | flops | bytes accessed | tf_op | source)
XLA Modules:
  0.0 68.7 jit_solution(11889201931661728130)
XLA Ops:
  0.6 0.0 copy-start
  0.6 1.6 %copy-done = bf16[128,8192]{1,0:T(8,128)(2,1)S(1)} copy-done((bf16[128,8192]{1,0:T(8,128)(2,1)S(1)}, bf16[128,8192]{1,0:T(8,128)(2,1)}, u32[]{:S(2)}) %copy-start) | copy-done | bytes 2097176
  2.2 0.0 copy-start.1
  2.2 0.8 %copy-done.1 = f32[8192]{0:T(1024)S(1)} copy-done((f32[8192]{0:T(1024)S(1)}, f32[8192]{0:T(1024)}, u32[]{:S(2)}) %copy-start.1) | copy-done | bytes 32792
  3.0 0.0 copy-start.2
  3.0 0.8 %copy-done.2 = s32[8192]{0:T(1024)S(1)} copy-done((s32[8192]{0:T(1024)S(1)}, s32[8192]{0:T(1024)}, u32[]{:S(2)}) %copy-start.2) | copy-done | bytes 32792
  3.7 0.0 copy-start.3
  3.7 0.7 %copy-done.3 = f32[4096]{0:T(1024)S(1)} copy-done((f32[4096]{0:T(1024)S(1)}, f32[4096]{0:T(1024)}, u32[]{:S(2)}) %copy-start.3) | copy-done | bytes 16408
  4.5 0.0 copy-start.4
  4.5 0.7 %copy-done.4 = f32[4096]{0:T(1024)S(1)} copy-done((f32[4096]{0:T(1024)S(1)}, f32[4096]{0:T(1024)}, u32[]{:S(2)}) %copy-start.4) | copy-done | bytes 16408
  5.2 0.0 copy-start.5
  5.2 0.7 copy-done.5
  5.9 0.0 copy-start.6
  5.9 0.7 copy-done.6
  6.5 0.0 copy-start.7
  6.5 0.7 copy-done.7
  7.2 0.0 copy-start.8
  7.2 0.7 copy-done.8
  7.8 58.8 %shard_map.120 = (f32[1,32]{1,0:T(1,128)S(1)}, f32[1,32]{1,0:T(1,128)S(1)}, f32[1,32]{1,0:T(1,128)S(1)}, f32[1,32]{1,0:T(1,128)S(1)}) custom-call(bf16[128,8192]{1,0:T(8,128)(2,1)S(1)} %copy-done, f32[1,8192]{1,0:T(1,128)S(1)} %bitcast.12, s32[1,8192]{1,0:T(1,128)S(1)} %bitcast.13, s32[2,128]{1,0:T(2,128)S(1)} %bitcast.16, f32[1,128]{1,0:T(1,128)S(1)} %bitcast.17, ...), custom_call_target="tpu_custom_call" | custom-call | tf_op jit(solution)/shard_map/pallas_call | solution.py:250
  66.6 0.5 copy.17
  67.1 0.5 copy.18
  67.6 0.5 copy.19
  68.1 0.5 copy.20
Async XLA Ops:
  0.6 1.6 %copy-start = (bf16[128,8192]{1,0:T(8,128)(2,1)S(1)}, bf16[128,8192]{1,0:T(8,128)(2,1)}, u32[]{:S(2)}) copy-start(bf16[128,8192]{1,0:T(8,128)(2,1)} %noise.1) | copy-start | bytes 6291460
  2.2 0.8 %copy-start.1 = (f32[8192]{0:T(1024)S(1)}, f32[8192]{0:T(1024)}, u32[]{:S(2)}) copy-start(f32[8192]{0:T(1024)} %param.10) | copy-start | bytes 98308
  3.0 0.8 %copy-start.2 = (s32[8192]{0:T(1024)S(1)}, s32[8192]{0:T(1024)}, u32[]{:S(2)}) copy-start(s32[8192]{0:T(1024)} %param.11) | copy-start | bytes 98308
  3.7 0.7 %copy-start.3 = (f32[4096]{0:T(1024)S(1)}, f32[4096]{0:T(1024)}, u32[]{:S(2)}) copy-start(f32[4096]{0:T(1024)} %param.15) | copy-start | bytes 49156
  4.5 0.7 %copy-start.4 = (f32[4096]{0:T(1024)S(1)}, f32[4096]{0:T(1024)}, u32[]{:S(2)}) copy-start(f32[4096]{0:T(1024)} %param.16) | copy-start | bytes 49156
  5.2 0.7 copy-start.5
  5.9 0.7 copy-start.6
  6.5 0.7 copy-start.7
  7.2 0.7 copy-start.8

commit v2 on v1

--- a/solution.py
+++ b/solution.py
@@ -11,17 +11,21 @@
 LANES = 128
 LOW = 256
 GROUP = 16
-CHUNK = 1024
-LAG = 1
+CHUNK = 4096
+SPLIT = 2
+LAG = 3
 
 
 def kernel(
-    axes, noise, insured, policy, bands, peak, year, deductible, limit, levels,
-    annual_out, occurrence_out, aggregate_out, excess_out,
-    block_mask, column_mask, center, inverse, strength, own, arrived, net_sum, halves, rows,
-    annual_all, occurrence_all,
-    send_sem, recv_sem, half_send, half_recv, row_send, row_recv,
+    axes, *refs
 ):
+    sources, (result,), inputs, rest = refs[:9], refs[9:10], refs[10:19], refs[19:]
+    noise, insured, policy, bands, peak, year, deductible, limit, levels = inputs
+    (
+        block_mask, column_mask, center, inverse, strength, own, arrived, net_sum, halves, rows,
+        annual_all, occurrence_all,
+        send_sem, recv_sem, half_send, half_recv, row_send, row_recv, load_sem,
+    ) = rest
     depth, owners = axes
     z = lax.axis_index("loc")
     ev = lax.axis_index("ev")
@@ -31,7 +35,16 @@
     half_blocks = blocks // 2
     groups = events // GROUP
     chunks = locations // CHUNK
-    half_rows = half_blocks * GROUP
+    piece_blocks = half_blocks // SPLIT
+    piece_rows = piece_blocks * GROUP
+    pieces = groups * SPLIT
+
+    loads = [
+        pltpu.make_async_copy(source, target, load_sem.at[i])
+        for i, (source, target) in enumerate(zip(sources, inputs))
+    ]
+    for i in (2, 3, 4, 0, 1, 5, 6, 7, 8):
+        loads[i].start()
 
     barrier = pltpu.get_barrier_semaphore()
     for k in range(1, depth):
@@ -39,6 +52,8 @@
     for k in range(1, owners):
         pl.semaphore_signal(barrier, inc=1, device_id={"ev": lax.rem(ev + k, owners)})
 
+    for i in (2, 3, 4):
+        loads[i].wait()
     low = jnp.transpose(jnp.broadcast_to(bands[0:1, :].astype(jnp.float32), (LANES, events)))
     high = jnp.transpose(jnp.broadcast_to(bands[1:2, :].astype(jnp.float32), (LANES, events)))
     center[...] = 0.5 * (low + high)
@@ -59,6 +74,8 @@
         return carry
 
     lax.fori_loop(0, chunks, build, 0)
+    for i in (0, 1, 5, 6, 7, 8):
+        loads[i].wait()
     pl.semaphore_wait(barrier, depth - 1 + owners - 1)
 
     anchor = z * locations
@@ -86,8 +103,10 @@
             )
 
         total = lax.fori_loop(0, chunks, part, jnp.zeros((blocks * GROUP, LOW), jnp.float32))
-        own[0, g] = total[:half_rows]
-        own[1, g] = total[half_rows:]
+        for d in (0, 1):
+            for j in range(SPLIT):
+                top_row = (d * SPLIT + j) * piece_rows
+                own[d, g * SPLIT + j] = total[top_row : top_row + piece_rows]
 
     def hop(d, g, there):
         return pltpu.make_async_remote_copy(
@@ -96,43 +115,45 @@
             device_id={"loc": there},
         )
 
-    def settle(d, g):
+    def settle(d, j, q):
         total = jnp.zeros((GROUP, LANES), jnp.float32)
-        for b in range(half_blocks):
-            for j in range(LOW // LANES):
-                row = (d * half_blocks + b) * (LOW // LANES) + j
-                gross = own[d, g, b * GROUP : (b + 1) * GROUP, j * LANES : (j + 1) * LANES]
+        for b in range(piece_blocks):
+            for i in range(LOW // LANES):
+                row = ((d * SPLIT + j) * piece_blocks + b) * (LOW // LANES) + i
+                gross = own[d, q, b * GROUP : (b + 1) * GROUP, i * LANES : (i + 1) * LANES]
                 net = jnp.maximum(gross - deductible[row : row + 1, :], 0.0)
                 total = total + jnp.minimum(net, limit[row : row + 1, :])
-        net_sum[pl.ds(pl.multiple_of(g * GROUP, GROUP), GROUP), :] = total
+        at = pl.multiple_of((q // SPLIT) * GROUP, GROUP)
+        net_sum[j, pl.ds(at, GROUP), :] = total
 
     def step(s, carry):
         @pl.when(s < groups)
         def _():
             compute(s)
 
-        for d in (0, 1):
-            gone = z if d == 1 else depth - 1 - z
-            there = jnp.minimum(z + 1, depth - 1) if d == 1 else jnp.maximum(z - 1, 0)
-            g = s - LAG * gone
-            active = (g >= 0) & (g < groups)
-
-            @pl.when(active & (gone > 0))
-            def _():
-                hop(d, g, there).wait_recv()
-                own[d, g] = own[d, g] + arrived[d, g]
-
-            @pl.when(active & (gone < depth - 1))
-            def _():
-                hop(d, g, there).start()
-
-            @pl.when(active & (gone == depth - 1))
-            def _():
-                settle(d, g)
+        for j in range(SPLIT):
+            for d in (0, 1):
+                gone = z if d == 1 else depth - 1 - z
+                there = jnp.minimum(z + 1, depth - 1) if d == 1 else jnp.maximum(z - 1, 0)
+                q = s * SPLIT + j - LAG * gone
+                active = (q >= 0) & (q < pieces)
+
+                @pl.when(active & (gone > 0))
+                def _():
+                    hop(d, q, there).wait_recv()
+                    own[d, q] = own[d, q] + arrived[d, q]
+
+                @pl.when(active & (gone < depth - 1))
+                def _():
+                    hop(d, q, there).start()
+
+                @pl.when(active & (gone == depth - 1))
+                def _():
+                    settle(d, (j - LAG * (depth - 1)) % SPLIT, q)
 
         return carry
 
-    lax.fori_loop(0, groups + LAG * (depth - 1), step, 0)
+    lax.fori_loop(0, groups + (LAG * (depth - 1) + SPLIT - 1) // SPLIT, step, 0)
 
     def half_copy(d, k):
         return pltpu.make_async_remote_copy(
@@ -146,7 +167,7 @@
 
         @pl.when(z == owner)
         def _():
-            row = jnp.sum(jnp.transpose(net_sum[...]), axis=0, keepdims=True)
+            row = jnp.sum(jnp.transpose(sum(net_sum[j] for j in range(SPLIT))), axis=0, keepdims=True)
             halves[d] = jnp.broadcast_to(row, (8, events))
             for k in range(1, depth):
                 half_copy(d, k).start()
@@ -199,16 +220,16 @@
 
     zero = jnp.zeros(levels.shape, jnp.float32)
     sums = lax.fori_loop(0, years // span, tally, (zero, zero))
-    aggregate_out[...] = sums[0] / years
-    excess_out[...] = sums[1] / years
+    result[2:3, : levels.shape[1]] = sums[0] / years
+    result[3:4, : levels.shape[1]] = sums[1] / years
 
     mine = pl.ds(pl.multiple_of(ev * YR_DEV, YR_DEV), YR_DEV)
     diagonal = lax.broadcasted_iota(jnp.int32, (YR_DEV, LANES), 0) == lax.broadcasted_iota(
         jnp.int32, (YR_DEV, LANES), 1
     )
-    for out, every in ((annual_out, annual_all), (occurrence_out, occurrence_all)):
+    for i, every in enumerate((annual_all, occurrence_all)):
         row = jnp.sum(jnp.where(diagonal, every[mine, :], 0.0), axis=0, keepdims=True)
-        out[...] = row[:, :YR_DEV]
+        result[i : i + 1, :] = row
 
     def drain(g, carry):
         for d in (0, 1):
@@ -220,7 +241,7 @@
 
         return carry
 
-    lax.fori_loop(0, groups, drain, 0)
+    lax.fori_loop(0, pieces, drain, 0)
     for d in (0, 1):
         owner = 0 if d == 0 else depth - 1
 
@@ -242,40 +263,10 @@
     thresholds = levels.shape[0]
     blocks = policies // LOW
     groups = events // GROUP
-    half_rows = blocks // 2 * GROUP
+    pieces = groups * SPLIT
+    piece_rows = blocks // 2 // SPLIT * GROUP
     years = YR_DEV * owners
-    row = jax.ShapeDtypeStruct((1, YR_DEV), jnp.float32)
-    curve = jax.ShapeDtypeStruct((1, thresholds), jnp.float32)
-    vmem = pl.BlockSpec(memory_space=pltpu.VMEM)
-    outs = pl.pallas_call(
-        functools.partial(kernel, (depth, owners)),
-        out_shape=(row, row, curve, curve),
-        in_specs=[vmem] * 9,
-        out_specs=(vmem,) * 4,
-        scratch_shapes=[
-            pltpu.VMEM((blocks * GROUP, locations), jnp.bfloat16),
-            pltpu.VMEM((LOW, locations), jnp.bfloat16),
-            pltpu.VMEM((events, LANES), jnp.float32),
-            pltpu.VMEM((events, LANES), jnp.float32),
-            pltpu.VMEM((events, LANES), jnp.float32),
-            pltpu.VMEM((2, groups, half_rows, LOW), jnp.float32),
-            pltpu.VMEM((2, groups, half_rows, LOW), jnp.float32),
-            pltpu.VMEM((events, LANES), jnp.float32),
-            pltpu.VMEM((2, 8, events), jnp.float32),
-            pltpu.VMEM((owners, 8, events), jnp.float32),
-            pltpu.VMEM((years, LANES), jnp.float32),
-            pltpu.VMEM((years, LANES), jnp.float32),
-            pltpu.SemaphoreType.DMA((2, groups)),
-            pltpu.SemaphoreType.DMA((2, groups)),
-            pltpu.SemaphoreType.DMA((depth,)),
-            pltpu.SemaphoreType.DMA((2,)),
-            pltpu.SemaphoreType.DMA((owners,)),
-            pltpu.SemaphoreType.DMA((owners,)),
-        ],
-        compiler_params=pltpu.CompilerParams(
-            collective_id=0, has_side_effects=True, vmem_limit_bytes=48 * 1024 * 1024
-        ),
-    )(
+    operands = (
         damage_noise,
         insured_value.reshape(1, locations),
         policy_id.reshape(1, locations),
@@ -286,7 +277,38 @@
         limit.reshape(policies // LANES, LANES),
         levels.reshape(1, thresholds),
     )
-    return tuple(out.reshape(-1) for out in outs)
+    out = pl.pallas_call(
+        functools.partial(kernel, (depth, owners)),
+        out_shape=jax.ShapeDtypeStruct((8, LANES), jnp.float32),
+        in_specs=[pl.BlockSpec(memory_space=pltpu.HBM)] * 9,
+        out_specs=pl.BlockSpec(memory_space=pltpu.VMEM),
+        scratch_shapes=[pltpu.VMEM(operand.shape, operand.dtype) for operand in operands]
+        + [
+            pltpu.VMEM((blocks * GROUP, locations), jnp.bfloat16),
+            pltpu.VMEM((LOW, locations), jnp.bfloat16),
+            pltpu.VMEM((events, LANES), jnp.float32),
+            pltpu.VMEM((events, LANES), jnp.float32),
+            pltpu.VMEM((events, LANES), jnp.float32),
+            pltpu.VMEM((2, pieces, piece_rows, LOW), jnp.float32),
+            pltpu.VMEM((2, pieces, piece_rows, LOW), jnp.float32),
+            pltpu.VMEM((SPLIT, events, LANES), jnp.float32),
+            pltpu.VMEM((2, 8, events), jnp.float32),
+            pltpu.VMEM((owners, 8, events), jnp.float32),
+            pltpu.VMEM((years, LANES), jnp.float32),
+            pltpu.VMEM((years, LANES), jnp.float32),
+            pltpu.SemaphoreType.DMA((2, pieces)),
+            pltpu.SemaphoreType.DMA((2, pieces)),
+            pltpu.SemaphoreType.DMA((depth,)),
+            pltpu.SemaphoreType.DMA((2,)),
+            pltpu.SemaphoreType.DMA((owners,)),
+            pltpu.SemaphoreType.DMA((owners,)),
+            pltpu.SemaphoreType.DMA((9,)),
+        ],
+        compiler_params=pltpu.CompilerParams(
+            collective_id=0, has_side_effects=True, vmem_limit_bytes=62 * 1024 * 1024
+        ),
+    )(*operands)
+    return out[0, :YR_DEV], out[1, :YR_DEV], out[2, :thresholds], out[3, :thresholds]
 
 
 def solution(mesh):

time: 69.1 us -> 50.6 us (0.73)
  Pallas kernels: 58.8 us -> 48.4 us
  local copies, waits for them, and re-layouts: 9.22 us -> 1.35 us
    pallas_call x1, Pallas kernels: 58.8 us -> 48.4 us  [local(): pl.pallas_call(functools.partial(kernel, (depth, owners)), out_shape=jax....]
    unnamed x22 -> x0, local copies, waits for them, and re-layouts: 9.22 us -> none
    squeeze x0 -> x1, local copies, waits for them, and re-layouts: none -> 1.35 us  [local(): out[3, :thresholds]]
where the time goes in v2:
time: 50.6 us; the launch traced here: 50.4 us
  Pallas kernels  48.4 us (96%)
  local copies, waits for them, and re-layouts  1.35 us (3%)
  between operations  0.64 us (1%)
    pallas_call x1, Pallas kernels, local(): pl.pallas_call(functools.partial(kernel, (depth, owners)), out_shape=jax....  48.4 us
    squeeze x1, local copies, waits for them, and re-layouts, local(): out[3, :thresholds]  1.35 us

profile of v2, /device:TPU:0, one launch (start us, length us, event | category | flops | bytes accessed | tf_op | source)
XLA Modules:
  0.0 50.4 jit_solution(10892075356027773700)
XLA Ops:
  0.6 48.4 %shard_map.120 = f32[8,128]{1,0:T(8,128)} custom-call(bf16[128,8192]{1,0:T(8,128)(2,1)} %refs_0_.1, f32[1,8192]{1,0:T(1,128)} %bitcast.16, s32[1,8192]{1,0:T(1,128)} %bitcast.17, s32[2,128]{1,0:T(2,128)} %bitcast.20, f32[1,128]{1,0:T(1,128)} %bitcast.21, s32[1,128]{1,0:T(1,128)} %bitcast.22, f32[32,128]{1,0:T(8,128)} %bitcast.18, f32[32,128]{1,0:T(8,128)} %bitcast.19, ...), custom_call_target="tpu_custom_call" | custom-call | tf_op jit(solution)/shard_map/pallas_call | solution.py:280
  49.1 1.3 %slice_bitcast_fusion = (f32[32]{0:T(128)}, f32[32]{0:T(128)}, f32[32]{0:T(128)}, f32[32]{0:T(128)}) fusion(f32[8,128]{1,0:T(8,128)} %shard_map.120), kind=kLoop, calls=%fused_computation | loop fusion | bytes 1024 | tf_op jit(solution)/shard_map/squeeze | solution.py:311
